TPU v7x, 32 devices: a whole 2x2x4 slice. The times are simulated.
32 devices in a mesh: grp: 8 (over y, x, core), tile: 4 (over z).
Axes of the slice: x: 2, y: 2, z: 4, core: 2. Of those that a mesh axis runs over, the one named last changes fastest.
Arguments:
- log_cond: float32 [8, 32, 32, 128], P('grp', 'tile'), may hold values from -3 to 3
- potential: float32 [8, 32, 32, 128], P('grp', 'tile'), may hold values from -6 to 6
- noise: float32 [2, 8, 32, 32, 128], P(None, 'grp', 'tile'), may hold values from -3 to 3
- source: float32 [32, 32, 128], P('tile'), may hold values from -6 to 6
- parents: int32 [8], replicated, may hold values from 0 to 7
- accept: int32 [2, 8], P(None, 'grp'), may hold values 0 or 1
- weights: float32 [8], P('grp'), may hold values from 0.1 to 10
Outputs:
- conduct_out: float32 [8, 32, 32, 128], P('grp', 'tile')
- potential_out: float32 [8, 32, 32, 128], P('grp', 'tile')
- moments: float32 [1024, 1024], P('tile')
Inputs may be any that keep to these rules, and one draw needn't show every extreme that they name: `parents`: parent indices of offspring.
All inputs are finite; a program needn't handle non-finite values. No bound on the sum of `accept` on one device may be relied on, other than what follows from the above.
Results may differ from a plain program's by a relative error of at most 0.0001.
Values sent between devices are 32-bit elements; how exact they have to be, the bound alone decides.
No kernel may reach another device: no remote copies, remote signals or barrier semaphores. Data moves between devices by JAX's collectives and lax.ppermute only.
A program may use at most 64 MiB of HBM per device.

v0:
```python
import jax
import jax.numpy as jnp
from jax import lax
from jax.sharding import PartitionSpec as P

prior_keep = 0.8
prior_fresh = 0.6
relax_weight = 0.8


def with_halo(block, sides, width):
    for axis, dim in sides:
        count = lax.axis_size(axis)
        forward = [(i, i + 1) for i in range(count - 1)]
        backward = [(target, source) for source, target in forward]
        low = lax.ppermute(
            lax.slice_in_dim(block, block.shape[dim] - width, None, axis=dim), axis, forward
        )
        high = lax.ppermute(lax.slice_in_dim(block, 0, width, axis=dim), axis, backward)
        block = jnp.concatenate([low, block, high], axis=dim)
    return block


def neighbours(padded):
    return [
        padded[2:, 1:-1, 1:-1],
        padded[:-2, 1:-1, 1:-1],
        padded[1:-1, 2:, 1:-1],
        padded[1:-1, :-2, 1:-1],
        padded[1:-1, 1:-1, 2:],
        padded[1:-1, 1:-1, :-2],
    ]


def relax_sweep(cond_ext, pot_ext, source):
    cond_pad = jnp.pad(cond_ext, ((0, 0), (1, 1), (1, 1)))
    pot_pad = jnp.pad(pot_ext, ((0, 0), (1, 1), (1, 1)))
    conductivity = jnp.exp(cond_pad)
    centre_k = conductivity[1:-1, 1:-1, 1:-1]
    centre = pot_pad[1:-1, 1:-1, 1:-1]
    flux_sum = jnp.zeros_like(centre)
    coef_sum = jnp.zeros_like(centre)
    for near_k, near_v in zip(neighbours(conductivity), neighbours(pot_pad)):
        face = 0.5 * (centre_k + near_k)
        flux_sum = flux_sum + face * near_v
        coef_sum = coef_sum + face
    return (1.0 - relax_weight) * centre + relax_weight * (source + flux_sum) / coef_sum


def local(log_cond, potential, noise, source, parents, accept, weights):
    mine = lax.axis_index("grp")
    bundle = jnp.stack([log_cond[0], potential[0]])
    parent = parents[mine]
    pieces = lax.all_gather(bundle[None], "grp", axis=0, tiled=True)
    owners = jnp.arange(pieces.shape[0], dtype=jnp.int32)
    chosen = jnp.where((owners == parent)[:, None, None, None, None], pieces, 0.0)
    moved = jnp.sum(chosen, axis=0)
    conduct = moved[0]
    pot = moved[1]
    width = conduct.shape[0]
    for move_index in range(noise.shape[0]):
        proposal = prior_keep * conduct + prior_fresh * noise[move_index, 0]
        extended = with_halo(jnp.stack([proposal, pot]), (("tile", 1),), 1)
        relaxed_once = relax_sweep(extended[0], extended[1], source)
        pot_ext = with_halo(relaxed_once, (("tile", 0),), 1)
        relaxed_twice = relax_sweep(extended[0], pot_ext, source)
        accepted = accept[move_index, 0] > 0
        conduct = jnp.where(accepted, proposal, conduct)
        pot = jnp.where(accepted, relaxed_twice, pot)
    weight_sum = lax.psum(jnp.sum(weights), "grp")
    share = weights[0] / weight_sum
    traces = jnp.transpose(pot, (1, 0, 2)).reshape(pot.shape[1], width * pot.shape[2])
    rows_here = traces.shape[1] // lax.axis_size("tile")
    own_start = lax.axis_index("tile") * rows_here
    piece = lax.all_gather(traces, "tile", axis=0, tiled=True)
    columns = lax.dynamic_slice_in_dim(piece, own_start, rows_here, 1)
    product = lax.dot_general(
        columns,
        piece,
        (((0,), (0,)), ((), ())),
        precision=lax.Precision.HIGHEST,
        preferred_element_type=jnp.float32,
    )
    partial_rows = share * product
    moments = lax.psum(partial_rows, "grp")
    return (conduct[None], pot[None], moments)


def solution(mesh):
    placed = (
        P("grp", "tile", None, None),
        P("grp", "tile", None, None),
        P(None, "grp", "tile", None, None),
        P("tile", None, None),
        P(),
        P(None, "grp"),
        P("grp"),
    )
    return jax.shard_map(
        local,
        mesh=mesh,
        in_specs=placed,
        out_specs=(P("grp", "tile", None, None), P("grp", "tile", None, None), P("tile", None)),
        check_vma=False,
    )
```

profile of v0, /device:TPU:0, one launch (start us, length us, event | category | flops | bytes accessed | tf_op | source)
XLA Modules:
  0.0 173.1 jit_solution(17961325413050397448)
XLA Ops:
  7.2 1.7 pad_maximum_fusion.2
  9.0 1.3 fusion.101
  11.6 1.2 dynamic_slice.6
  12.9 0.6 iota_compare_fusion.4
  13.5 27.6 %all-gather.3.cloned.1.call-done = f32[16,8,32,128]{3,2,1,0:T(8,128)} async-done(((f32[2,8,32,128]{3,2,1,0:T(8,128)}), f32[16,8,32,128]{3,2,1,0:T(8,128)}) %all-gather.3.cloned.1.call-update) | async-done | bytes 2097168 | tf_op jit(solution)/shard_map/all_gather | solution.py:54
  41.1 2.0 %select_reduce_fusion = f32[2,8,32,128]{3,2,1,0:T(8,128)S(1)} fusion(f32[8,2,8,32,128]{4,3,2,1,0:T(8,128)} %bitcast.65, pred[8]{0:T(512)(128)(4,1)S(1)} %iota_compare_fusion.4), kind=kLoop, calls=%fused_computation | loop fusion | flops 983040 | bytes 2359304 | tf_op jit(solution)/shard_map/reduce_sum | solution.py:57
  43.1 0.7 broadcast_select_fusion
  43.8 3.4 %collective-permute-start = (f32[2,1,32,128]{3,2,1,0:T(8,128)S(1)}, f32[2,1,32,128]{3,2,1,0:T(8,128)S(1)}, u32[]{:S(2)}, u32[]{:S(2)}) collective-permute-start(f32[2,1,32,128]{3,2,1,0:T(8,128)S(1)} %get-tuple-element.12), channel_id=1, source_target_pairs={{0,1},{1,2},{2,3},{4,5},{5,6},{6,7},{8,9},{9,10},{10,11},{12,13},{... | collective-permute-start | bytes 98312 | tf_op jit(solution)/shard_map/ppermute | solution.py:16
  47.2 1.3 collective-permute-start.1
  48.8 4.2 %collective-permute-done.1 = f32[2,1,32,128]{3,2,1,0:T(8,128)S(1)} collective-permute-done((f32[2,1,32,128]{3,2,1,0:T(8,128)S(1)}, f32[2,1,32,128]{3,2,1,0:T(8,128)S(1)}, u32[]{:S(2)}, u32[]{:S(2)}) %collective-permute-start.1) | collective-permute-done | bytes 32800 | tf_op jit(solution)/shard_map/ppermute | solution.py:19
  53.3 1.3 collective-permute-start.2
  54.6 4.5 %collective-permute-start.3 = (f32[1,32,128]{2,1,0:T(8,128)S(1)}, f32[1,32,128]{2,1,0:T(8,128)S(1)}, u32[]{:S(2)}, u32[]{:S(2)}) collective-permute-start(f32[1,32,128]{2,1,0:T(8,128)S(1)} %get-tuple-element.17), channel_id=1, source_target_pairs={{0,1},{1,2},{2,3},{4,5},{5,6},{6,7},{8,9},{9,10},{10,11},{12,13},{... | collective-permute-start | bytes 49160 | tf_op jit(solution)/shard_map/ppermute | solution.py:16
  59.2 1.4 collective-permute-done.3
  60.8 0.3 fusion.83
  61.1 4.2 %collective-permute-start.4 = (f32[2,1,32,128]{3,2,1,0:T(8,128)S(1)}, f32[2,1,32,128]{3,2,1,0:T(8,128)S(1)}, u32[]{:S(2)}, u32[]{:S(2)}) collective-permute-start(f32[2,1,32,128]{3,2,1,0:T(8,128)S(1)} %get-tuple-element.10), channel_id=1, source_target_pairs={{0,1},{1,2},{2,3},{4,5},{5,6},{6,7},{8,9},{9,10},{10,11},{12,13},{... | collective-permute-start | bytes 98312 | tf_op jit(solution)/shard_map/ppermute | solution.py:16
  65.3 1.3 collective-permute-start.5
  66.9 4.2 %collective-permute-done.5 = f32[2,1,32,128]{3,2,1,0:T(8,128)S(1)} collective-permute-done((f32[2,1,32,128]{3,2,1,0:T(8,128)S(1)}, f32[2,1,32,128]{3,2,1,0:T(8,128)S(1)}, u32[]{:S(2)}, u32[]{:S(2)}) %collective-permute-start.5) | collective-permute-done | bytes 32800 | tf_op jit(solution)/shard_map/ppermute | solution.py:19
  71.5 1.3 collective-permute-start.6
  72.8 4.5 %collective-permute-start.7 = (f32[1,32,128]{2,1,0:T(8,128)S(1)}, f32[1,32,128]{2,1,0:T(8,128)S(1)}, u32[]{:S(2)}, u32[]{:S(2)}) collective-permute-start(f32[1,32,128]{2,1,0:T(8,128)S(1)} %get-tuple-element.15), channel_id=1, source_target_pairs={{0,1},{1,2},{2,3},{4,5},{5,6},{6,7},{8,9},{9,10},{10,11},{12,13},{... | collective-permute-start | bytes 49160 | tf_op jit(solution)/shard_map/ppermute | solution.py:16
  77.3 12.5 %psum.14 = f32[]{:T(128)} all-reduce(f32[]{:T(128)} %bitcast.17), channel_id=1, replica_groups=mesh['grp'=8,'tile'=4] {'grp'}, use_global_device_ids=true, to_apply=%region_1.2 | all-reduce | flops 1 | bytes 8 | tf_op jit(solution)/shard_map/psum | solution.py:70
  91.7 15.9 %all_gather.7 = f32[128,1024]{1,0:T(8,128)S(1)} all-gather(f32[32,1024]{1,0:T(8,128)S(1)} %copy_bitcast_fusion), channel_id=1, replica_groups=mesh['grp'=8,'tile'=4] {'tile'}, dimensions={0}, use_global_device_ids=true | all-gather | bytes 655360 | tf_op jit(solution)/shard_map/all_gather | solution.py:75
  107.6 2.0 %convolution_multiply_fusion = f32[256,1024]{1,0:T(8,128)} fusion(f32[128,1024]{1,0:T(8,128)S(1)} %all_gather.7, f32[]{:T(128)S(6)} %div.19, s32[]{:T(128)S(6)} %select_n.49), kind=kOutput, calls=%fused_computation.1 | convolution fusion | flops 402915328 | bytes 1703944 | tf_op jit(solution)/shard_map/dot_general | solution.py:77
  109.6 54.4 %all-reduce.8.cloned.1.call-done = f32[256,1024]{1,0:T(8,128)} async-done(((f32[256,1024]{1,0:T(8,128)}), f32[256,1024]{1,0:T(8,128)}) %all-reduce.8.cloned.1.call-update) | async-done | bytes 1048592 | tf_op jit(solution)/shard_map/psum | solution.py:85
  164.0 2.3 %copy.16 = f32[256,1024]{1,0:T(8,128)} copy(f32[256,1024]{1,0:T(8,128)} %all-reduce.8.cloned.1.call-done) | data formatting | bytes 2097152
  (29 shorter events, 2.0 us)
Async XLA Ops:
  7.2 35.9 %copy-start.2 = (f32[2,1,8,32,128]{4,3,2,1,0:T(8,128)S(1)}, f32[2,1,8,32,128]{4,3,2,1,0:T(8,128)}, u32[]{:S(2)}) copy-start(f32[2,1,8,32,128]{4,3,2,1,0:T(8,128)} %param.9) | copy-start | bytes 786436
  7.2 33.9 %all-gather.3.cloned.1.call-start = ((), (), s32[]{:S(2)}) async-start(), calls=%async_computation.1 | async-start | bytes 2359296 | tf_op jit(solution)/shard_map/all_gather | solution.py:54
  9.0 155.0 %all-reduce.8.cloned.1.call-start = ((), (), s32[]{:S(2)}) async-start(), calls=%async_computation | async-start | bytes 2097152 | tf_op jit(solution)/shard_map/psum | solution.py:85
  41.1 12.0 %copy-start = (f32[8,32,128]{2,1,0:T(8,128)S(1)}, f32[8,32,128]{2,1,0:T(8,128)}, u32[]{:S(2)}) copy-start(f32[8,32,128]{2,1,0:T(8,128)} %param.10) | copy-start | bytes 393220
  43.8 5.0 %collective-permute-start = (f32[2,1,32,128]{3,2,1,0:T(8,128)S(1)}, f32[2,1,32,128]{3,2,1,0:T(8,128)S(1)}, u32[]{:S(2)}, u32[]{:S(2)}) collective-permute-start(f32[2,1,32,128]{3,2,1,0:T(8,128)S(1)} %get-tuple-element.12), channel_id=1, source_target_pairs={{0,1},{1,2},{2,3},{4,5},{5,6},{6,7},{8,9},{9,10},{10,11},{12,13},{... | collective-permute-start | bytes 98312 | tf_op jit(solution)/shard_map/ppermute | solution.py:16
  47.2 5.8 %collective-permute-start.1 = (f32[2,1,32,128]{3,2,1,0:T(8,128)S(1)}, f32[2,1,32,128]{3,2,1,0:T(8,128)S(1)}, u32[]{:S(2)}, u32[]{:S(2)}) collective-permute-start(f32[2,1,32,128]{3,2,1,0:T(8,128)S(1)} %get-tuple-element.13), channel_id=1, source_target_pairs={{1,0},{2,1},{3,2},{5,4},{6,5},{7,6},{9,8},{10,9},{11,10},{13,12},{... | collective-permute-start | bytes 98312 | tf_op jit(solution)/shard_map/ppermute | solution.py:19
  53.3 5.9 %collective-permute-start.2 = (f32[1,32,128]{2,1,0:T(8,128)S(1)}, f32[1,32,128]{2,1,0:T(8,128)S(1)}, u32[]{:S(2)}, u32[]{:S(2)}) collective-permute-start(f32[1,32,128]{2,1,0:T(8,128)S(1)} %get-tuple-element.18), channel_id=1, source_target_pairs={{1,0},{2,1},{3,2},{5,4},{6,5},{7,6},{9,8},{10,9},{11,10},{13,12},{... | collective-permute-start | bytes 49160 | tf_op jit(solution)/shard_map/ppermute | solution.py:19
  54.6 6.0 %collective-permute-start.3 = (f32[1,32,128]{2,1,0:T(8,128)S(1)}, f32[1,32,128]{2,1,0:T(8,128)S(1)}, u32[]{:S(2)}, u32[]{:S(2)}) collective-permute-start(f32[1,32,128]{2,1,0:T(8,128)S(1)} %get-tuple-element.17), channel_id=1, source_target_pairs={{0,1},{1,2},{2,3},{4,5},{5,6},{6,7},{8,9},{9,10},{10,11},{12,13},{... | collective-permute-start | bytes 49160 | tf_op jit(solution)/shard_map/ppermute | solution.py:16
  61.1 5.8 %collective-permute-start.4 = (f32[2,1,32,128]{3,2,1,0:T(8,128)S(1)}, f32[2,1,32,128]{3,2,1,0:T(8,128)S(1)}, u32[]{:S(2)}, u32[]{:S(2)}) collective-permute-start(f32[2,1,32,128]{3,2,1,0:T(8,128)S(1)} %get-tuple-element.10), channel_id=1, source_target_pairs={{0,1},{1,2},{2,3},{4,5},{5,6},{6,7},{8,9},{9,10},{10,11},{12,13},{... | collective-permute-start | bytes 98312 | tf_op jit(solution)/shard_map/ppermute | solution.py:16
  65.3 5.8 %collective-permute-start.5 = (f32[2,1,32,128]{3,2,1,0:T(8,128)S(1)}, f32[2,1,32,128]{3,2,1,0:T(8,128)S(1)}, u32[]{:S(2)}, u32[]{:S(2)}) collective-permute-start(f32[2,1,32,128]{3,2,1,0:T(8,128)S(1)} %get-tuple-element.11), channel_id=1, source_target_pairs={{1,0},{2,1},{3,2},{5,4},{6,5},{7,6},{9,8},{10,9},{11,10},{13,12},{... | collective-permute-start | bytes 98312 | tf_op jit(solution)/shard_map/ppermute | solution.py:19
  71.5 19.7 %collective-permute-start.6 = (f32[1,32,128]{2,1,0:T(8,128)S(1)}, f32[1,32,128]{2,1,0:T(8,128)S(1)}, u32[]{:S(2)}, u32[]{:S(2)}) collective-permute-start(f32[1,32,128]{2,1,0:T(8,128)S(1)} %get-tuple-element.16), channel_id=1, source_target_pairs={{1,0},{2,1},{3,2},{5,4},{6,5},{7,6},{9,8},{10,9},{11,10},{13,12},{... | collective-permute-start | bytes 49160 | tf_op jit(solution)/shard_map/ppermute | solution.py:19
  72.8 18.4 %collective-permute-start.7 = (f32[1,32,128]{2,1,0:T(8,128)S(1)}, f32[1,32,128]{2,1,0:T(8,128)S(1)}, u32[]{:S(2)}, u32[]{:S(2)}) collective-permute-start(f32[1,32,128]{2,1,0:T(8,128)S(1)} %get-tuple-element.15), channel_id=1, source_target_pairs={{0,1},{1,2},{2,3},{4,5},{5,6},{6,7},{8,9},{9,10},{10,11},{12,13},{... | collective-permute-start | bytes 49160 | tf_op jit(solution)/shard_map/ppermute | solution.py:16
  91.7 74.6 %copy-start.1 = (f32[8,32,128]{2,1,0:T(8,128)}, f32[8,32,128]{2,1,0:T(8,128)S(1)}, u32[]{:S(2)}) copy-start(f32[8,32,128]{2,1,0:T(8,128)S(1)} %fusion.64) | copy-start | bytes 393220
Sparse Core Ops, SparseCore 0:
  10.5 30.5 all-gather.2
  109.7 54.2 all-reduce.7
where the time goes:
time: 174 us; the launch traced here: 173 us
  waiting for transfers between devices  92.4 us (53%)
  blocking collectives  28.3 us (16%)
  starting transfers between devices  21.9 us (13%)
  between operations  16.9 us (10%)
  other arithmetic  6.59 us (4%)
  local copies, waits for them, and re-layouts  4.94 us (3%)
  matrix products  2.01 us (1%)
    psum x1, waiting for transfers between devices, local(): moments = lax.psum(partial_rows, 'grp')  54.4 us
    all_gather x1, waiting for transfers between devices, local(): pieces = lax.all_gather(bundle[None], 'grp', axis=0, tiled=True)  27.6 us
    ppermute x4, starting transfers between devices, with_halo(): lax.ppermute(lax.slice_in_dim(block, block.shape[dim] - width, None, axis...  16.7 us
    all_gather x1, blocking collectives, local(): piece = lax.all_gather(traces, 'tile', axis=0, tiled=True)  15.9 us
    psum x1, blocking collectives, local(): weight_sum = lax.psum(jnp.sum(weights), 'grp')  12.5 us
    ppermute x4, waiting for transfers between devices, with_halo(): lax.ppermute(lax.slice_in_dim(block, 0, width, axis=dim), axis, backward)  8.46 us
    ppermute x4, starting transfers between devices, with_halo(): lax.ppermute(lax.slice_in_dim(block, 0, width, axis=dim), axis, backward)  5.17 us
  transfers between devices with their start and end apart: 10, of which 7 were waited for; matrix products, arithmetic and copies ran while one was open for 2% of the time, Pallas kernels for 0%

commit v1 on v0

v1 whole, which is shorter than its diff:
```python
import functools

import jax
import jax.numpy as jnp
from jax import lax
from jax.experimental import pallas as pl
from jax.experimental.pallas import tpu as pltpu
from jax.sharding import PartitionSpec as P

prior_keep = 0.8
prior_fresh = 0.6
relax_weight = 0.8


def choose_kernel(parents_ref, pieces_ref, chosen_ref):
    for place in range(chosen_ref.shape[0]):
        chosen_ref[place] = pieces_ref[parents_ref[place]]


def choose(parents, pieces):
    return pl.pallas_call(
        choose_kernel,
        out_shape=jax.ShapeDtypeStruct(pieces.shape, pieces.dtype),
        in_specs=[
            pl.BlockSpec(memory_space=pltpu.SMEM),
            pl.BlockSpec(memory_space=pltpu.VMEM),
        ],
        out_specs=pl.BlockSpec(memory_space=pltpu.VMEM),
        name="choose",
    )(parents, pieces)


def exchange_halo(low_edge, high_edge):
    count = lax.axis_size("tile")
    forward = [(i, i + 1) for i in range(count - 1)]
    backward = [(target, source) for source, target in forward]
    low = lax.ppermute(high_edge, "tile", forward)
    high = lax.ppermute(low_edge, "tile", backward)
    return low, high


def neighbours(padded):
    return [
        padded[2:, 1:-1, 1:-1],
        padded[:-2, 1:-1, 1:-1],
        padded[1:-1, 2:, 1:-1],
        padded[1:-1, :-2, 1:-1],
        padded[1:-1, 1:-1, 2:],
        padded[1:-1, 1:-1, :-2],
    ]


def relax_sweep(cond_ext, pot_ext, source):
    cond_pad = jnp.pad(cond_ext, ((0, 0), (1, 1), (1, 1)))
    pot_pad = jnp.pad(pot_ext, ((0, 0), (1, 1), (1, 1)))
    conductivity = jnp.exp(cond_pad)
    centre_k = conductivity[1:-1, 1:-1, 1:-1]
    centre = pot_pad[1:-1, 1:-1, 1:-1]
    flux_sum = jnp.zeros_like(centre)
    coef_sum = jnp.zeros_like(centre)
    for near_k, near_v in zip(neighbours(conductivity), neighbours(pot_pad)):
        face = 0.5 * (centre_k + near_k)
        flux_sum = flux_sum + face * near_v
        coef_sum = coef_sum + face
    return (1.0 - relax_weight) * centre + relax_weight * (source + flux_sum) / coef_sum


def inside(block, halo, width):
    if halo == 0:
        return block
    tile = lax.axis_index("tile")
    layer = lax.broadcasted_iota(jnp.int32, (block.shape[0], 1, 1), 0)
    low_ok = (tile > 0) | (layer >= halo)
    high_ok = (tile < lax.axis_size("tile") - 1) | (layer < halo + width)
    return jnp.where(low_ok & high_ok, block, 0.0)


def local(log_cond, potential, noise, source, parents, accept, weights):
    moves = noise.shape[0]
    width, ny, nz = source.shape
    reach = 2 * moves
    particles = lax.axis_size("grp")

    fixed = [noise[m, 0] for m in range(moves)] + [source]
    depth = [reach - 2 * m for m in range(moves)] + [reach - 1]
    low_fixed, high_fixed = exchange_halo(
        jnp.concatenate([field[:h] for field, h in zip(fixed, depth)]),
        jnp.concatenate([field[width - h:] for field, h in zip(fixed, depth)]),
    )
    wide = []
    at = 0
    for field, h in zip(fixed, depth):
        wide.append(jnp.concatenate([low_fixed[at:at + h], field, high_fixed[at:at + h]]))
        at += h
    noise_wide, source_wide = wide[:moves], wide[moves]

    bundle = jnp.stack([log_cond[0], potential[0]])
    rows = bundle.size // (particles * nz)
    pieces = jnp.concatenate(
        [
            bundle.reshape(particles, rows, nz),
            jnp.broadcast_to(weights[0], (particles, 8, nz)),
        ],
        axis=1,
    )
    pieces = lax.all_to_all(pieces, "grp", 0, 0, tiled=True)
    share = weights[0] / jnp.sum(pieces[:, rows, 0])
    moved = lax.all_to_all(choose(parents, pieces[:, :rows]), "grp", 0, 0, tiled=True)
    moved = moved.reshape(2, width, ny, nz)

    low, high = exchange_halo(moved[:, :reach], moved[:, width - reach:])
    extended = jnp.concatenate([low, moved, high], axis=1)
    conduct, pot = extended[0], extended[1]

    halo = reach
    for m in range(moves):
        proposal = prior_keep * conduct + prior_fresh * noise_wide[m]
        once = relax_sweep(proposal, pot, source_wide[reach - halo:source_wide.shape[0] - reach + halo])
        once = inside(once, halo - 1, width)
        twice = relax_sweep(
            proposal[1:-1], once,
            source_wide[reach - halo + 1:source_wide.shape[0] - reach + halo - 1],
        )
        twice = inside(twice, halo - 2, width)
        accepted = accept[m, 0] > 0
        conduct = jnp.where(accepted, proposal, conduct)[2:-2]
        pot = jnp.where(accepted, twice, pot[2:-2])
        halo -= 2

    traces = jnp.transpose(pot, (1, 0, 2)).reshape(ny, width * nz)
    rows_here = traces.shape[1] // lax.axis_size("tile")
    own_start = lax.axis_index("tile") * rows_here
    piece = lax.all_gather(traces, "tile", axis=0, tiled=True)
    columns = lax.dynamic_slice_in_dim(piece, own_start, rows_here, 1)
    product = lax.dot_general(
        columns,
        piece,
        (((0,), (0,)), ((), ())),
        precision=lax.Precision.HIGHEST,
        preferred_element_type=jnp.float32,
    )
    partial_rows = share * product
    parts = lax.all_to_all(
        partial_rows.reshape(particles, rows_here // particles, -1), "grp", 0, 0, tiled=True
    )
    moments = lax.all_gather(jnp.sum(parts, axis=0), "grp", axis=0, tiled=True)
    return (conduct[None], pot[None], moments)


def solution(mesh):
    placed = (
        P("grp", "tile", None, None),
        P("grp", "tile", None, None),
        P(None, "grp", "tile", None, None),
        P("tile", None, None),
        P(),
        P(None, "grp"),
        P("grp"),
    )
    return jax.shard_map(
        local,
        mesh=mesh,
        in_specs=placed,
        out_specs=(P("grp", "tile", None, None), P("grp", "tile", None, None), P("tile", None)),
        check_vma=False,
    )
```

time: 174 us -> 123 us (0.71)
  waiting for transfers between devices: 92.4 us -> 34.9 us
  local copies, waits for them, and re-layouts: 4.94 us -> 10.6 us
  blocking collectives: 28.3 us -> 33.8 us
  other arithmetic: 6.59 us -> 3.73 us
  starting transfers between devices: 21.9 us -> 19.5 us
    psum x1 -> x0, waiting for transfers between devices: 54.4 us -> none  [local(): moments = lax.psum(partial_rows, 'grp')]
    all_to_all x0 -> x1, blocking collectives: none -> 17.8 us  [local(): lax.all_to_all(partial_rows.reshape(particles, rows_here // particles, -1...]
    all_to_all x0 -> x2, waiting for transfers between devices: none -> 12.8 us  [the longest x1 6.78 us: local(): lax.all_to_all(choose(parents, pieces[:, :rows]), 'grp', 0, 0, tiled=True)]
    psum x1 -> x0, blocking collectives: 12.5 us -> none  [local(): weight_sum = lax.psum(jnp.sum(weights), 'grp')]
    ppermute x8 -> x4, starting transfers between devices: 21.8 us -> 11.8 us  [the longest x2 9.18 us: exchange_halo(): low = lax.ppermute(high_edge, 'tile', forward)]
    ppermute x8 -> x4, waiting for transfers between devices: 10.4 us -> 1.63 us  [the longest x2 1.62 us: exchange_halo(): high = lax.ppermute(low_edge, 'tile', backward)]
    all_to_all x0 -> x2, starting transfers between devices: none -> 7.7 us  [the longest x1 4.16 us: local(): pieces = lax.all_to_all(pieces, 'grp', 0, 0, tiled=True)]
    all_gather x1, waiting for transfers between devices: 27.6 us -> 20.5 us  [local(): moments = lax.all_gather(jnp.sum(parts, axis=0), 'grp', axis=0, tiled=True)]
  transfers between devices with their start and end apart: 10 -> 7, of which waited for: 7 -> 4; matrix products, arithmetic and copies ran while one was open for 2% -> 3% of each run, Pallas kernels for 0% -> 1%
where the time goes in v1:
time: 123 us; the launch traced here: 122 us
  waiting for transfers between devices  34.9 us (28%)
  blocking collectives  33.8 us (27%)
  starting transfers between devices  19.5 us (16%)
  between operations  16.9 us (14%)
  local copies, waits for them, and re-layouts  10.6 us (9%)
  other arithmetic  3.73 us (3%)
  Pallas kernels  1.67 us (1%)
    all_gather x1, waiting for transfers between devices, local(): moments = lax.all_gather(jnp.sum(parts, axis=0), 'grp', axis=0, tiled=True)  20.5 us
    all_to_all x1, blocking collectives, local(): lax.all_to_all(partial_rows.reshape(particles, rows_here // particles, -1...  17.8 us
    all_gather x1, blocking collectives, local(): piece = lax.all_gather(traces, 'tile', axis=0, tiled=True)  16 us
    ppermute x2, starting transfers between devices, exchange_halo(): low = lax.ppermute(high_edge, 'tile', forward)  9.18 us
    all_to_all x1, waiting for transfers between devices, local(): lax.all_to_all(choose(parents, pieces[:, :rows]), 'grp', 0, 0, tiled=True)  6.78 us
    all_to_all x1, waiting for transfers between devices, local(): pieces = lax.all_to_all(pieces, 'grp', 0, 0, tiled=True)  6.04 us
    unnamed x17, local copies, waits for them, and re-layouts  4.94 us
    all_to_all x1, starting transfers between devices, local(): pieces = lax.all_to_all(pieces, 'grp', 0, 0, tiled=True)  4.16 us
  transfers between devices with their start and end apart: 7, of which 4 were waited for; matrix products, arithmetic and copies ran while one was open for 3% of the time, Pallas kernels for 1%

profile of v1, /device:TPU:0, one launch (start us, length us, event | category | flops | bytes accessed | tf_op | source)
XLA Modules:
  0.0 122.2 jit_solution(14234259080105606283)
XLA Ops:
  7.2 0.8 slice_bitcast_fusion.10
  8.0 0.9 slice_bitcast_fusion.8
  8.9 1.3 %collective-permute-start.3 = (f32[9,32,128]{2,1,0:T(8,128)S(1)}, f32[9,32,128]{2,1,0:T(8,128)S(1)}, u32[]{:S(2)}, u32[]{:S(2)}) collective-permute-start(f32[9,32,128]{2,1,0:T(8,128)S(1)} %pad_maximum_fusion.4), channel_id=1, source_target_pairs={{1,0},{2,1},{3,2},{5,4},{6,5},{7,6},{9,8},{10,9},{11,10},{13,12},{... | collective-permute-start | bytes 442376 | tf_op jit(solution)/shard_map/ppermute | solution.py:38
  10.3 5.7 %collective-permute-start.2 = (f32[9,32,128]{2,1,0:T(8,128)S(1)}, f32[9,32,128]{2,1,0:T(8,128)S(1)}, u32[]{:S(2)}, u32[]{:S(2)}) collective-permute-start(f32[9,32,128]{2,1,0:T(8,128)S(1)} %pad_maximum_fusion.3), channel_id=1, source_target_pairs={{0,1},{1,2},{2,3},{4,5},{5,6},{6,7},{8,9},{9,10},{10,11},{12,13},{... | collective-permute-start | bytes 442376 | tf_op jit(solution)/shard_map/ppermute | solution.py:37
  16.7 0.7 concatenate.21
  17.4 4.2 %all-to-all-start = ((f32[8,72,128]{2,1,0:T(8,128)}), f32[8,72,128]{2,1,0:T(8,128)S(1)}, u32[]{:S(2)}, u32[]{:S(2)}) async-start(f32[8,72,128]{2,1,0:T(8,128)} %concatenate.21), calls=%async_computation | async-start | bytes 589824 | tf_op jit(solution)/shard_map/all_to_all | solution.py:106
  22.8 6.0 %all-to-all-done = f32[8,72,128]{2,1,0:T(8,128)S(1)} async-done(((f32[8,72,128]{2,1,0:T(8,128)}), f32[8,72,128]{2,1,0:T(8,128)S(1)}, u32[]{:S(2)}, u32[]{:S(2)}) %all-to-all-start) | async-done | bytes 294944 | tf_op jit(solution)/shard_map/all_to_all | solution.py:106
  28.9 0.7 slice.393.pieces_ref
  29.6 1.7 %choose.1 = f32[8,64,128]{2,1,0:T(8,128)} custom-call(s32[8]{0:T(128)} %parents_ref.1, f32[8,64,128]{2,1,0:T(8,128)} %slice.393.pieces_ref), custom_call_target="tpu_custom_call" | custom-call | tf_op jit(solution)/shard_map/choose/pallas_call | solution.py:21
  31.3 3.5 %all-to-all-start.1 = ((f32[8,64,128]{2,1,0:T(8,128)}), f32[8,64,128]{2,1,0:T(8,128)S(1)}, u32[]{:S(2)}, u32[]{:S(2)}) async-start(f32[8,64,128]{2,1,0:T(8,128)} %choose.1), calls=%async_computation.1 | async-start | bytes 524288 | tf_op jit(solution)/shard_map/all_to_all | solution.py:108
  34.9 6.8 %all-to-all-done.1 = f32[8,64,128]{2,1,0:T(8,128)S(1)} async-done(((f32[8,64,128]{2,1,0:T(8,128)}), f32[8,64,128]{2,1,0:T(8,128)S(1)}, u32[]{:S(2)}, u32[]{:S(2)}) %all-to-all-start.1) | async-done | bytes 262176 | tf_op jit(solution)/shard_map/all_to_all | solution.py:108
  41.7 3.5 %collective-permute-start = (f32[2,4,32,128]{3,2,1,0:T(8,128)S(1)}, f32[2,4,32,128]{3,2,1,0:T(8,128)S(1)}, u32[]{:S(2)}, u32[]{:S(2)}) collective-permute-start(f32[2,4,32,128]{3,2,1,0:T(8,128)S(1)} %get-tuple-element.11), channel_id=1, source_target_pairs={{0,1},{1,2},{2,3},{4,5},{5,6},{6,7},{8,9},{9,10},{10,11},{12,13},{... | collective-permute-start | bytes 393224 | tf_op jit(solution)/shard_map/ppermute | solution.py:37
  45.2 1.3 %collective-permute-start.1 = (f32[2,4,32,128]{3,2,1,0:T(8,128)S(1)}, f32[2,4,32,128]{3,2,1,0:T(8,128)S(1)}, u32[]{:S(2)}, u32[]{:S(2)}) collective-permute-start(f32[2,4,32,128]{3,2,1,0:T(8,128)S(1)} %get-tuple-element.12), channel_id=1, source_target_pairs={{1,0},{2,1},{3,2},{5,4},{6,5},{7,6},{9,8},{10,9},{11,10},{13,12},{... | collective-permute-start | bytes 393224 | tf_op jit(solution)/shard_map/ppermute | solution.py:38
  47.8 0.7 copy-done.3
  50.4 1.6 %collective-permute-done.1 = f32[2,4,32,128]{3,2,1,0:T(8,128)S(1)} collective-permute-done((f32[2,4,32,128]{3,2,1,0:T(8,128)S(1)}, f32[2,4,32,128]{3,2,1,0:T(8,128)S(1)}, u32[]{:S(2)}, u32[]{:S(2)}) %collective-permute-start.1) | collective-permute-done | bytes 131104 | tf_op jit(solution)/shard_map/ppermute | solution.py:38
  52.2 0.8 slice-done.2
  53.0 0.7 slice-done.1
  56.3 16.0 %all_gather.6 = f32[128,1024]{1,0:T(8,128)S(1)} all-gather(f32[32,1024]{1,0:T(8,128)S(1)} %copy_bitcast_fusion), channel_id=1, replica_groups=mesh['grp'=8,'tile'=4] {'tile'}, dimensions={0}, use_global_device_ids=true | all-gather | bytes 655360 | tf_op jit(solution)/shard_map/all_gather | solution.py:133
  72.3 1.0 convolution_multiply_fusion
  73.4 17.8 %all_to_all.15 = f32[8,32,1024]{2,1,0:T(8,128)S(1)} all-to-all(f32[8,32,1024]{2,1,0:T(8,128)S(1)} %bitcast.64), channel_id=1, replica_groups=mesh['grp'=8,'tile'=4] {'grp'}, dimensions={0} | all-to-all | bytes 2097152 | tf_op jit(solution)/shard_map/all_to_all | solution.py:143
  91.2 0.7 reduce_sum.19
  91.9 0.7 fusion.133
  92.6 20.5 %all-gather.2.cloned.1.call-done = f32[256,1024]{1,0:T(8,128)} async-done(((f32[32,1024]{1,0:T(8,128)}), f32[256,1024]{1,0:T(8,128)}) %all-gather.2.cloned.1.call-update) | async-done | bytes 1048592 | tf_op jit(solution)/shard_map/all_gather | solution.py:146
  113.0 2.3 %copy.15 = f32[256,1024]{1,0:T(8,128)} copy(f32[256,1024]{1,0:T(8,128)} %all-gather.2.cloned.1.call-done) | data formatting | bytes 2097152
  (49 shorter events, 5.4 us)
Async XLA Ops:
  7.9 1.0 copy-start
  8.9 38.9 %collective-permute-start.3 = (f32[9,32,128]{2,1,0:T(8,128)S(1)}, f32[9,32,128]{2,1,0:T(8,128)S(1)}, u32[]{:S(2)}, u32[]{:S(2)}) collective-permute-start(f32[9,32,128]{2,1,0:T(8,128)S(1)} %pad_maximum_fusion.4), channel_id=1, source_target_pairs={{1,0},{2,1},{3,2},{5,4},{6,5},{7,6},{9,8},{10,9},{11,10},{13,12},{... | collective-permute-start | bytes 442376 | tf_op jit(solution)/shard_map/ppermute | solution.py:38
  10.2 6.4 %copy-start.5 = (f32[1,8,32,128]{3,2,1,0:T(8,128)S(1)}, f32[1,8,32,128]{3,2,1,0:T(8,128)}, u32[]{:S(2)}) copy-start(f32[1,8,32,128]{3,2,1,0:T(8,128)} %param.8) | copy-start | bytes 393220
  10.3 6.4 %copy-start.6 = (f32[1,8,32,128]{3,2,1,0:T(8,128)S(1)}, f32[1,8,32,128]{3,2,1,0:T(8,128)}, u32[]{:S(2)}) copy-start(f32[1,8,32,128]{3,2,1,0:T(8,128)} %param.7) | copy-start | bytes 393220
  10.3 38.2 %collective-permute-start.2 = (f32[9,32,128]{2,1,0:T(8,128)S(1)}, f32[9,32,128]{2,1,0:T(8,128)S(1)}, u32[]{:S(2)}, u32[]{:S(2)}) collective-permute-start(f32[9,32,128]{2,1,0:T(8,128)S(1)} %pad_maximum_fusion.3), channel_id=1, source_target_pairs={{0,1},{1,2},{2,3},{4,5},{5,6},{6,7},{8,9},{9,10},{10,11},{12,13},{... | collective-permute-start | bytes 442376 | tf_op jit(solution)/shard_map/ppermute | solution.py:37
  17.4 11.4 %all-to-all-start = ((f32[8,72,128]{2,1,0:T(8,128)}), f32[8,72,128]{2,1,0:T(8,128)S(1)}, u32[]{:S(2)}, u32[]{:S(2)}) async-start(f32[8,72,128]{2,1,0:T(8,128)} %concatenate.21), calls=%async_computation | async-start | bytes 589824 | tf_op jit(solution)/shard_map/all_to_all | solution.py:106
  21.6 0.7 copy-start.7
  31.3 3.6 %copy-start.1 = (f32[2,1,8,32,128]{4,3,2,1,0:T(8,128)S(1)}, f32[2,1,8,32,128]{4,3,2,1,0:T(8,128)}, u32[]{:S(2)}) copy-start(f32[2,1,8,32,128]{4,3,2,1,0:T(8,128)} %param.9) | copy-start | bytes 786436
  31.3 10.4 %all-to-all-start.1 = ((f32[8,64,128]{2,1,0:T(8,128)}), f32[8,64,128]{2,1,0:T(8,128)S(1)}, u32[]{:S(2)}, u32[]{:S(2)}) async-start(f32[8,64,128]{2,1,0:T(8,128)} %choose.1), calls=%async_computation.1 | async-start | bytes 524288 | tf_op jit(solution)/shard_map/all_to_all | solution.py:108
  34.8 78.2 %all-gather.2.cloned.1.call-start = ((), (), s32[]{:S(2)}) async-start(), calls=%async_computation.3 | async-start | bytes 1179648 | tf_op jit(solution)/shard_map/all_gather | solution.py:146
  41.7 8.7 %collective-permute-start = (f32[2,4,32,128]{3,2,1,0:T(8,128)S(1)}, f32[2,4,32,128]{3,2,1,0:T(8,128)S(1)}, u32[]{:S(2)}, u32[]{:S(2)}) collective-permute-start(f32[2,4,32,128]{3,2,1,0:T(8,128)S(1)} %get-tuple-element.11), channel_id=1, source_target_pairs={{0,1},{1,2},{2,3},{4,5},{5,6},{6,7},{8,9},{9,10},{10,11},{12,13},{... | collective-permute-start | bytes 393224 | tf_op jit(solution)/shard_map/ppermute | solution.py:37
  45.2 6.9 %collective-permute-start.1 = (f32[2,4,32,128]{3,2,1,0:T(8,128)S(1)}, f32[2,4,32,128]{3,2,1,0:T(8,128)S(1)}, u32[]{:S(2)}, u32[]{:S(2)}) collective-permute-start(f32[2,4,32,128]{3,2,1,0:T(8,128)S(1)} %get-tuple-element.12), channel_id=1, source_target_pairs={{1,0},{2,1},{3,2},{5,4},{6,5},{7,6},{9,8},{10,9},{11,10},{13,12},{... | collective-permute-start | bytes 393224 | tf_op jit(solution)/shard_map/ppermute | solution.py:38
  47.8 0.7 copy-start.3
  48.5 0.7 copy-start.4
  52.1 0.8 slice-start.2
  52.1 0.9 slice-start.5
  53.0 0.8 slice-start.1
  53.0 0.8 slice-start.4
  53.8 0.8 slice-start
  53.8 0.8 slice-start.3
  55.7 0.7 copy-start.2
Sparse Core Ops, SparseCore 0:
  92.0 20.9 all-gather.1

commit v2 on v0

v2 whole, which is shorter than its diff:
```python
import functools

import jax
import jax.numpy as jnp
from jax import lax
from jax.experimental import pallas as pl
from jax.experimental.pallas import tpu as pltpu
from jax.sharding import PartitionSpec as P

prior_keep = 0.8
prior_fresh = 0.6
relax_weight = 0.8

SMEM = pl.BlockSpec(memory_space=pltpu.SMEM)
VMEM = pl.BlockSpec(memory_space=pltpu.VMEM)
ANY = pl.BlockSpec(memory_space=pl.ANY)


def in_vmem(array):
    return pltpu.with_memory_space_constraint(array, pltpu.VMEM)


def pack_kernel(rows, weight_ref, cond_ref, pot_ref, out_ref, sems):
    copies = []
    for piece in range(out_ref.shape[0]):
        row = piece * rows
        field = cond_ref if row < cond_ref.shape[0] else pot_ref
        row %= cond_ref.shape[0]
        copies.append(
            pltpu.make_async_copy(
                field.at[pl.ds(row, rows)], out_ref.at[piece, pl.ds(0, rows)], sems.at[piece]
            )
        )
    for copy in copies:
        copy.start()
    weight = jnp.full((8, out_ref.shape[2]), weight_ref[0], jnp.float32)
    for piece in range(out_ref.shape[0]):
        out_ref[piece, rows:rows + 8] = weight
    for copy in copies:
        copy.wait()


def pack(weights, log_cond, potential, particles):
    nz = log_cond.shape[-1]
    rows = 2 * log_cond.size // (particles * nz)
    return pl.pallas_call(
        functools.partial(pack_kernel, rows),
        out_shape=pltpu.VMEM((particles, rows + 8, nz), jnp.float32),
        in_specs=[SMEM, ANY, ANY],
        out_specs=VMEM,
        scratch_shapes=[pltpu.SemaphoreType.DMA((particles,))],
        name="pack",
    )(weights, log_cond.reshape(-1, nz), potential.reshape(-1, nz))


def choose_kernel(parents_ref, weight_ref, pieces_ref, chosen_ref, root_ref):
    rows = chosen_ref.shape[1]
    for place in range(chosen_ref.shape[0]):
        chosen_ref[place] = pieces_ref[parents_ref[place], pl.ds(0, rows)]
    total = pieces_ref[0, rows:rows + 8]
    for place in range(1, pieces_ref.shape[0]):
        total += pieces_ref[place, rows:rows + 8]
    root_ref[...] = jnp.sqrt(weight_ref[0] / total)


def choose(parents, weights, pieces):
    particles, rows, nz = pieces.shape
    return pl.pallas_call(
        choose_kernel,
        out_shape=(
            pltpu.VMEM((particles, rows - 8, nz), jnp.float32),
            pltpu.VMEM((8, nz), jnp.float32),
        ),
        in_specs=[SMEM, SMEM, VMEM],
        out_specs=(VMEM, VMEM),
        name="choose",
    )(parents, weights, in_vmem(pieces))


def six_sum(before, here, after, edge):
    row = lax.broadcasted_iota(jnp.int32, here.shape, 0)
    lane = lax.broadcasted_iota(jnp.int32, here.shape, 1)
    ny, nz = here.shape
    down = jnp.where(row == 0, edge, pltpu.roll(here, 1, 0))
    up = jnp.where(row == ny - 1, edge, pltpu.roll(here, ny - 1, 0))
    left = jnp.where(lane == 0, edge, pltpu.roll(here, 1, 1))
    right = jnp.where(lane == nz - 1, edge, pltpu.roll(here, nz - 1, 1))
    return ((before + after) + (down + up)) + (left + right)


def moves_kernel(
    depth, accept_ref, root_ref, moved_ref, low_ref, high_ref, noise_ref, source_ref,
    cond_out, pot_out, traces_out, cond, pot, once, conductivity, gain,
):
    moves, width, _, nz = noise_ref.shape
    reach = 2 * moves
    span = width + 2 * reach
    tile = lax.axis_index("tile")
    first = tile == 0
    last = tile == lax.axis_size("tile") - 1

    def fetch(field, at, h, i):
        if i < 0:
            return low_ref[at + h + i]
        if i >= width:
            return high_ref[at + i - width]
        return field[i]

    def keep_inside(value, i):
        outside = (first & (i < reach)) | (last & (i >= reach + width))
        return jnp.where(outside, 0.0, value)

    for i in range(span):
        cond[i] = fetch(moved_ref.at[0], 0, reach, i - reach)
        pot[i] = fetch(moved_ref.at[1], reach, reach, i - reach)

    source_at = 2 * reach + sum(depth[:moves])
    for m in range(moves):
        start = 2 * m
        noise_at = 2 * reach + sum(depth[:m])
        accepted = accept_ref[m, 0] > 0

        def sweep(old, lo, hi):
            for i in range(lo, hi):
                here, here_k = old[i], conductivity[i]
                before, after = old[i - 1], old[i + 1]
                plain = six_sum(before, here, after, 0.0)
                scaled = six_sum(
                    before * conductivity[i - 1], here * here_k, after * conductivity[i + 1], 0.0
                )
                source = fetch(source_ref, source_at, reach - 1, i - reach)
                value = (1.0 - relax_weight) * here + (
                    2.0 * source + (here_k * plain + scaled)
                ) * gain[i]
                yield i, keep_inside(value, i)

        for i in range(start, span - start):
            proposal = prior_keep * cond[i] + prior_fresh * fetch(
                noise_ref.at[m], noise_at, depth[m], i - reach
            )
            conductivity[i] = jnp.exp(proposal)
            cond[i] = jnp.where(accepted, proposal, cond[i])
        for i in range(start + 1, span - start - 1):
            here_k = conductivity[i]
            gain[i] = relax_weight / (
                6.0 * here_k + six_sum(conductivity[i - 1], here_k, conductivity[i + 1], 1.0)
            )
        for i, value in sweep(pot, start + 1, span - start - 1):
            once[i] = value
        for i, value in sweep(once, start + 2, span - start - 2):
            pot[i] = jnp.where(accepted, value, pot[i])

    root = root_ref[0:1]
    for i in range(width):
        cond_out[i] = cond[i + reach]
        value = pot[i + reach]
        pot_out[i] = value
        traces_out[:, i * nz:(i + 1) * nz] = value * root


def run_moves(depth, accept, root, moved, low, high, noise, source):
    moves, width, ny, nz = noise.shape
    span = width + 4 * moves
    return pl.pallas_call(
        functools.partial(moves_kernel, depth),
        out_shape=(
            pltpu.VMEM((width, ny, nz), jnp.float32),
            pltpu.VMEM((width, ny, nz), jnp.float32),
            pltpu.VMEM((ny, width * nz), jnp.float32),
        ),
        in_specs=[SMEM] + [VMEM] * 6,
        out_specs=(VMEM, VMEM, VMEM),
        scratch_shapes=[pltpu.VMEM((span, ny, nz), jnp.float32)] * 5,
        name="moves",
    )(accept, root, *[in_vmem(a) for a in (moved, low, high, noise, source)])


def exchange_halo(low_edge, high_edge):
    count = lax.axis_size("tile")
    forward = [(i, i + 1) for i in range(count - 1)]
    backward = [(target, source) for source, target in forward]
    low = lax.ppermute(high_edge, "tile", forward)
    high = lax.ppermute(low_edge, "tile", backward)
    return low, high


def local(log_cond, potential, noise, source, parents, accept, weights):
    moves = noise.shape[0]
    width, ny, nz = source.shape
    reach = 2 * moves
    particles = lax.axis_size("grp")

    pieces = pack(weights, log_cond, potential, particles)
    pieces = lax.all_to_all(pieces, "grp", 0, 0, tiled=True)
    chosen, root = choose(parents, weights, pieces)
    moved = lax.all_to_all(chosen, "grp", 0, 0, tiled=True).reshape(2, width, ny, nz)

    fields = [moved[0], moved[1]] + [noise[m, 0] for m in range(moves)] + [source]
    depth = [reach, reach] + [reach - 2 * m for m in range(moves)] + [reach - 1]
    low, high = exchange_halo(
        jnp.concatenate([field[:h] for field, h in zip(fields, depth)]),
        jnp.concatenate([field[width - h:] for field, h in zip(fields, depth)]),
    )
    conduct, pot, traces = run_moves(
        tuple(depth[2:]), accept, root, moved, low, high, noise[:, 0], source
    )

    rows_here = traces.shape[1] // lax.axis_size("tile")
    own_start = lax.axis_index("tile") * rows_here
    piece = lax.all_gather(traces, "tile", axis=0, tiled=True)
    columns = lax.dynamic_slice_in_dim(piece, own_start, rows_here, 1)
    product = lax.dot_general(
        columns,
        piece,
        (((0,), (0,)), ((), ())),
        precision=lax.Precision.HIGHEST,
        preferred_element_type=jnp.float32,
    )
    parts = lax.all_to_all(
        product.reshape(particles, rows_here // particles, -1), "grp", 0, 0, tiled=True
    )
    mine = jnp.sum(parts, axis=0)
    copies = jnp.broadcast_to(mine, (particles,) + mine.shape)
    moments = lax.all_to_all(copies, "grp", 0, 0, tiled=True).reshape(rows_here, -1)
    return (conduct[None], pot[None], moments)


def solution(mesh):
    placed = (
        P("grp", "tile", None, None),
        P("grp", "tile", None, None),
        P(None, "grp", "tile", None, None),
        P("tile", None, None),
        P(),
        P(None, "grp"),
        P("grp"),
    )
    return jax.shard_map(
        local,
        mesh=mesh,
        in_specs=placed,
        out_specs=(P("grp", "tile", None, None), P("grp", "tile", None, None), P("tile", None)),
        check_vma=False,
    )
```

time: 174 us -> 96.3 us (0.55)
  waiting for transfers between devices: 92.4 us -> 17.7 us
  blocking collectives: 28.3 us -> 56.3 us
  between operations: 16.9 us -> 1.42 us
  starting transfers between devices: 21.9 us -> 9.41 us
  other arithmetic: 6.59 us -> 0.06 us
  Pallas kernels: 0 us -> 3.41 us
    psum x1 -> x0, waiting for transfers between devices: 54.4 us -> none  [local(): moments = lax.psum(partial_rows, 'grp')]
    all_to_all x0 -> x3, blocking collectives: none -> 39.4 us  [the longest x1 17.8 us: local(): lax.all_to_all(product.reshape(particles, rows_here // particles, -1), 'g...]
    all_gather x1 -> x0, waiting for transfers between devices: 27.6 us -> none  [local(): pieces = lax.all_gather(bundle[None], 'grp', axis=0, tiled=True)]
    ppermute x8 -> x2, starting transfers between devices: 21.8 us -> 5.86 us  [the longest x1 4.56 us: exchange_halo(): low = lax.ppermute(high_edge, 'tile', forward)]
    all_to_all x0 -> x1, waiting for transfers between devices: none -> 14 us  [local(): lax.all_to_all(copies, 'grp', 0, 0, tiled=True).reshape(rows_here, -1)]
    psum x1 -> x0, blocking collectives: 12.5 us -> none  [local(): weight_sum = lax.psum(jnp.sum(weights), 'grp')]
    ppermute x8 -> x2, waiting for transfers between devices: 10.4 us -> 3.64 us  [the longest x1 2.46 us: exchange_halo(): high = lax.ppermute(low_edge, 'tile', backward)]
    all_to_all x0 -> x1, starting transfers between devices: none -> 3.56 us  [local(): lax.all_to_all(copies, 'grp', 0, 0, tiled=True).reshape(rows_here, -1)]
  transfers between devices with their start and end apart: 10 -> 3, of which waited for: 7 -> 3; matrix products, arithmetic and copies ran while one was open for 2% -> 2% of each run, Pallas kernels for 0% -> 0%
where the time goes in v2:
time: 96.3 us; the launch traced here: 95.8 us
  blocking collectives  56.3 us (58%)
  waiting for transfers between devices  17.7 us (18%)
  starting transfers between devices  9.41 us (10%)
  local copies, waits for them, and re-layouts  6.53 us (7%)
  Pallas kernels  3.41 us (4%)
  between operations  1.42 us (1%)
  matrix products  1.03 us (1%)
    all_to_all x1, blocking collectives, local(): lax.all_to_all(product.reshape(particles, rows_here // particles, -1), 'g...  17.8 us
    all_gather x1, blocking collectives, local(): piece = lax.all_gather(traces, 'tile', axis=0, tiled=True)  16.9 us
    all_to_all x1, waiting for transfers between devices, local(): lax.all_to_all(copies, 'grp', 0, 0, tiled=True).reshape(rows_here, -1)  14 us
    all_to_all x1, blocking collectives, local(): pieces = lax.all_to_all(pieces, 'grp', 0, 0, tiled=True)  12.3 us
    all_to_all x1, blocking collectives, local(): lax.all_to_all(chosen, 'grp', 0, 0, tiled=True).reshape(2, width, ny, nz)  9.35 us
    unnamed x17, local copies, waits for them, and re-layouts  5.41 us
    ppermute x1, starting transfers between devices, exchange_halo(): low = lax.ppermute(high_edge, 'tile', forward)  4.56 us
    all_to_all x1, starting transfers between devices, local(): lax.all_to_all(copies, 'grp', 0, 0, tiled=True).reshape(rows_here, -1)  3.56 us
  transfers between devices with their start and end apart: 3, of which 3 were waited for; matrix products, arithmetic and copies ran while one was open for 2% of the time, Pallas kernels for 0%

profile of v2, /device:TPU:0, one launch (start us, length us, event | category | flops | bytes accessed | tf_op | source)
XLA Modules:
  0.0 95.8 jit_solution(9634543711110276849)
XLA Ops:
  1.3 0.9 pack.1
  2.2 12.3 %all_to_all.20.pieces_ref = f32[8,72,128]{2,1,0:T(8,128)S(1)} all-to-all(f32[8,72,128]{2,1,0:T(8,128)S(1)} %pack.1), channel_id=1, replica_groups=mesh['grp'=8,'tile'=4] {'grp'}, dimensions={0} | all-to-all | bytes 589824 | tf_op jit(solution)/shard_map/all_to_all | solution.py:194
  14.5 0.7 choose.1
  15.2 0.0 copy-start.2
  15.2 9.3 %all_to_all.21 = f32[8,64,128]{2,1,0:T(8,128)S(1)} all-to-all(f32[8,64,128]{2,1,0:T(8,128)S(1)} %get-tuple-element.9), channel_id=1, replica_groups=mesh['grp'=8,'tile'=4] {'grp'}, dimensions={0} | all-to-all | bytes 524288 | tf_op jit(solution)/shard_map/all_to_all | solution.py:196
  24.6 0.9 copy-done
  25.6 0.9 copy-done.1
  26.4 1.3 %collective-permute-start.1 = (f32[17,32,128]{2,1,0:T(8,128)S(1)}, f32[17,32,128]{2,1,0:T(8,128)S(1)}, u32[]{:S(2)}, u32[]{:S(2)}) collective-permute-start(f32[17,32,128]{2,1,0:T(8,128)S(1)} %get-tuple-element.21), channel_id=1, source_target_pairs={{1,0},{2,1},{3,2},{5,4},{6,5},{7,6},{9,8},{10,9},{11,10},{13,12},{... | collective-permute-start | bytes 835592 | tf_op jit(solution)/shard_map/ppermute | solution.py:183
  27.7 4.6 %collective-permute-start = (f32[17,32,128]{2,1,0:T(8,128)S(1)}, f32[17,32,128]{2,1,0:T(8,128)S(1)}, u32[]{:S(2)}, u32[]{:S(2)}) collective-permute-start(f32[17,32,128]{2,1,0:T(8,128)S(1)} %get-tuple-element.22), channel_id=1, source_target_pairs={{0,1},{1,2},{2,3},{4,5},{5,6},{6,7},{8,9},{9,10},{10,11},{12,13},{... | collective-permute-start | bytes 835592 | tf_op jit(solution)/shard_map/ppermute | solution.py:182
  32.3 0.6 copy-done.3
  33.0 0.6 copy.10.accept_ref
  33.6 2.5 %collective-permute-done.1.high_ref = f32[17,32,128]{2,1,0:T(8,128)S(1)} collective-permute-done((f32[17,32,128]{2,1,0:T(8,128)S(1)}, f32[17,32,128]{2,1,0:T(8,128)S(1)}, u32[]{:S(2)}, u32[]{:S(2)}) %collective-permute-start.1) | collective-permute-done | bytes 278560 | tf_op jit(solution)/shard_map/ppermute | solution.py:183
  36.1 1.2 %collective-permute-done.low_ref = f32[17,32,128]{2,1,0:T(8,128)S(1)} collective-permute-done((f32[17,32,128]{2,1,0:T(8,128)S(1)}, f32[17,32,128]{2,1,0:T(8,128)S(1)}, u32[]{:S(2)}, u32[]{:S(2)}) %collective-permute-start) | collective-permute-done | bytes 278560 | tf_op jit(solution)/shard_map/ppermute | solution.py:182
  37.3 1.8 %moves.1 = (f32[8,32,128]{2,1,0:T(8,128)S(1)}, f32[8,32,128]{2,1,0:T(8,128)S(1)}, f32[32,1024]{1,0:T(8,128)S(1)}) custom-call(s32[2,1]{1,0:T(2,128)} %copy.10.accept_ref, f32[8,128]{1,0:T(8,128)} %copy-done.2, f32[2,8,32,128]{3,2,1,0:T(8,128)S(1)} %bitcast.23, f32[17,32,128]{2,1,0:T(8,128)S(1)} %collective-permute-done.low_ref, ...), custom_call_target="tpu_custom_call" | custom-call | tf_op jit(solution)/shard_map/moves/pallas_call | solution.py:164
  39.1 16.9 %all_gather.3 = f32[128,1024]{1,0:T(8,128)S(1)} all-gather(f32[32,1024]{1,0:T(8,128)S(1)} %get-tuple-element.12), channel_id=1, replica_groups=mesh['grp'=8,'tile'=4] {'tile'}, dimensions={0}, use_global_device_ids=true | all-gather | bytes 655360 | tf_op jit(solution)/shard_map/all_gather | solution.py:210
  56.0 1.0 %fusion = f32[256,1024]{1,0:T(8,128)S(1)} fusion(f32[128,1024]{1,0:T(8,128)S(1)} %all_gather.3, s32[]{:T(128)S(6)} %select_n.3), kind=kOutput, calls=%fused_computation | convolution fusion | flops 402653184 | bytes 1703940 | tf_op jit(solution)/shard_map/dot_general | solution.py:212
  57.0 17.8 %all_to_all.22 = f32[8,32,1024]{2,1,0:T(8,128)S(1)} all-to-all(f32[8,32,1024]{2,1,0:T(8,128)S(1)} %bitcast.26), channel_id=1, replica_groups=mesh['grp'=8,'tile'=4] {'grp'}, dimensions={0} | all-to-all | bytes 2097152 | tf_op jit(solution)/shard_map/all_to_all | solution.py:219
  74.8 0.1 reduce_sum.9
  74.9 1.1 %broadcast_in_dim.11 = f32[8,32,1024]{2,1,0:T(8,128)} broadcast(f32[32,1024]{1,0:T(8,128)S(1)} %reduce_sum.9), dimensions={1,2} | broadcast | bytes 1179648 | tf_op jit(solution)/shard_map/broadcast_in_dim | solution.py:223
  76.0 3.6 %all-to-all-start.3 = ((f32[8,32,1024]{2,1,0:T(8,128)}), f32[8,32,1024]{2,1,0:T(8,128)S(1)}, u32[]{:S(2)}, u32[]{:S(2)}) async-start(f32[8,32,1024]{2,1,0:T(8,128)} %broadcast_in_dim.11), calls=%async_computation.3 | async-start | bytes 2097152 | tf_op jit(solution)/shard_map/all_to_all | solution.py:224
  79.5 0.7 copy.20
  80.2 0.7 copy.21
  80.8 14.0 %all-to-all-done.3 = f32[8,32,1024]{2,1,0:T(8,128)S(1)} async-done(((f32[8,32,1024]{2,1,0:T(8,128)}), f32[8,32,1024]{2,1,0:T(8,128)S(1)}, u32[]{:S(2)}, u32[]{:S(2)}) %all-to-all-start.3) | async-done | bytes 1048608 | tf_op jit(solution)/shard_map/all_to_all | solution.py:224
  94.9 1.0 %copy.23 = f32[256,1024]{1,0:T(8,128)} copy(f32[256,1024]{1,0:T(8,128)S(1)} %bitcast.25) | data formatting | bytes 2097152
  (11 shorter events, 0.1 us)
Async XLA Ops:
  15.2 9.4 %copy-start.2 = (f32[8,128]{1,0:T(8,128)}, f32[8,128]{1,0:T(8,128)S(1)}, u32[]{:S(2)}) copy-start(f32[8,128]{1,0:T(8,128)S(1)} %get-tuple-element.8.root_ref) | copy-start | bytes 12292
  24.6 1.0 copy-start
  25.5 0.9 copy-start.1
  26.4 9.6 %collective-permute-start.1 = (f32[17,32,128]{2,1,0:T(8,128)S(1)}, f32[17,32,128]{2,1,0:T(8,128)S(1)}, u32[]{:S(2)}, u32[]{:S(2)}) collective-permute-start(f32[17,32,128]{2,1,0:T(8,128)S(1)} %get-tuple-element.21), channel_id=1, source_target_pairs={{1,0},{2,1},{3,2},{5,4},{6,5},{7,6},{9,8},{10,9},{11,10},{13,12},{... | collective-permute-start | bytes 835592 | tf_op jit(solution)/shard_map/ppermute | solution.py:183
  27.7 9.5 %collective-permute-start = (f32[17,32,128]{2,1,0:T(8,128)S(1)}, f32[17,32,128]{2,1,0:T(8,128)S(1)}, u32[]{:S(2)}, u32[]{:S(2)}) collective-permute-start(f32[17,32,128]{2,1,0:T(8,128)S(1)} %get-tuple-element.22), channel_id=1, source_target_pairs={{0,1},{1,2},{2,3},{4,5},{5,6},{6,7},{8,9},{9,10},{10,11},{12,13},{... | collective-permute-start | bytes 835592 | tf_op jit(solution)/shard_map/ppermute | solution.py:182
  32.3 0.7 copy-start.3
  76.0 18.9 %all-to-all-start.3 = ((f32[8,32,1024]{2,1,0:T(8,128)}), f32[8,32,1024]{2,1,0:T(8,128)S(1)}, u32[]{:S(2)}, u32[]{:S(2)}) async-start(f32[8,32,1024]{2,1,0:T(8,128)} %broadcast_in_dim.11), calls=%async_computation.3 | async-start | bytes 2097152 | tf_op jit(solution)/shard_map/all_to_all | solution.py:224
